TPU v7x, 1024 devices: a whole 4x8x16 slice. The times are simulated.
1024 devices in a mesh: dp: 16 (over z), ctx: 16 (over y_lo, x, core), tp: 4 (over y_hi).
Axes of the slice: x: 4, y: 8 (y_hi: 4, y_lo: 2; y = y_hi * 2 + y_lo), z: 16, core: 2. Of those that a mesh axis runs over, the one named last changes fastest.
Arguments:
- hidden: bfloat16 [393216, 768], P(('dp', 'ctx', 'tp')), may hold values from -24 to 24
- grad_output: bfloat16 [131072, 2048], P(('dp', 'ctx', 'tp')), may hold values from -6 to 6
- expert_ids: int32 [131072, 2], P(('dp', 'ctx', 'tp')), may hold values from 0 to 63, all different within a row; in each aligned block of 128 rows (0 to 127, 128 to 255, ...) at most 6 rows name the same one
- gate_weights: float32 [131072, 2], P(('dp', 'ctx', 'tp')), may hold values from 0.2 to 1
- w_down: bfloat16 [64, 768, 2048], P(('ctx', 'tp')), may hold values from -0.21875 to 0.21875
Outputs:
- combined: bfloat16 [131072, 2048], P(('dp', 'ctx', 'tp'))
- grad_hidden: bfloat16 [393216, 768], P(('dp', 'ctx', 'tp'))
- grad_down: bfloat16 [64, 768, 2048], P(('ctx', 'tp'), 'dp')
Inputs may be any that keep to these rules, and one draw needn't show every extreme that they name: `expert_ids`: each row names 2 different experts. Among the 128 rows of one device no expert is named more than 6 times, and in every draw some device names some expert exactly 6 times.
All inputs are finite; a program needn't handle non-finite values.
Results may differ from a plain program's by a relative error of at most 0.017.
Values may be sent and summed in bfloat16 or wider, within the bound.
A program may use at most 64 MiB of HBM per device.

v0:
```python
import jax
import jax.numpy as jnp
from jax import lax
from jax.sharding import PartitionSpec as P

grad_scale = 0.015625


def slot_index(ids_block, experts, capacity):
    flat_ids = ids_block.reshape(-1)
    one_hot = (flat_ids[:, None] == jnp.arange(experts, dtype=jnp.int32)[None, :]).astype(jnp.int32)
    earlier = jnp.cumsum(one_hot, axis=0) - one_hot
    ranking = jnp.sum(earlier * one_hot, axis=1)
    return flat_ids * capacity + ranking


def local(hidden, grad_output, expert_ids, gate_weights, w_down):
    ctx_count = lax.axis_size("ctx")
    tp_count = lax.axis_size("tp")
    experts = ctx_count * tp_count
    capacity = hidden.shape[0] // experts
    tok_rows, choices = expert_ids.shape
    model_width = grad_output.shape[1]
    weight = w_down[0]
    positions = slot_index(expert_ids, experts, capacity)
    expert_out = jnp.dot(hidden, weight, preferred_element_type=jnp.float32).astype(jnp.bfloat16)
    expert_out = expert_out.reshape(experts, capacity, model_width)
    returned = lax.all_to_all(expert_out, ("ctx", "tp"), split_axis=0, concat_axis=0, tiled=True)
    returned = returned.reshape(experts * capacity, model_width)
    picked = returned[positions].astype(jnp.float32).reshape(tok_rows, choices, model_width)
    combined = jnp.sum(gate_weights[:, :, None] * picked, axis=1).astype(jnp.bfloat16)
    scaled = (gate_weights[:, :, None] * grad_output[:, None, :].astype(jnp.float32)).astype(
        jnp.bfloat16
    )
    scaled = scaled.reshape(tok_rows * choices, model_width)
    outgoing = jnp.zeros((experts * capacity, model_width), jnp.bfloat16).at[positions].set(scaled)
    outgoing = outgoing.reshape(experts, capacity, model_width)
    incoming = lax.all_to_all(outgoing, ("ctx", "tp"), split_axis=0, concat_axis=0, tiled=True)
    incoming = incoming.reshape(experts * capacity, model_width)
    grad_hidden = lax.dot_general(
        incoming, weight, (((1,), (1,)), ((), ())), preferred_element_type=jnp.float32
    ).astype(jnp.bfloat16)
    summed = lax.psum_scatter(
        lax.dot_general(
            hidden, incoming, (((0,), (0,)), ((), ())), preferred_element_type=jnp.float32
        ).astype(jnp.bfloat16),
        "dp",
        scatter_dimension=0,
        tiled=True,
    ).astype(jnp.float32)
    grad_down = (summed * grad_scale).astype(jnp.bfloat16)[None]
    return (combined, grad_hidden, grad_down)


def solution(mesh):
    return jax.shard_map(
        local,
        mesh=mesh,
        in_specs=(
            P(("dp", "ctx", "tp"), None),
            P(("dp", "ctx", "tp"), None),
            P(("dp", "ctx", "tp"), None),
            P(("dp", "ctx", "tp"), None),
            P(("ctx", "tp"), None, None),
        ),
        out_specs=(
            P(("dp", "ctx", "tp"), None),
            P(("dp", "ctx", "tp"), None),
            P(("ctx", "tp"), "dp", None),
        ),
        check_vma=False,
    )
```

profile of v0, /device:TPU:1, one launch (start us, length us, event | category | flops | bytes accessed | tf_op | source)
XLA Modules:
  0.0 209.0 jit_solution(9849270324902340775)
XLA Ops:
  7.2 0.8 broadcast_multiply_fusion
  8.1 0.9 copy.19
  9.5 0.8 copy.17
  10.4 0.6 reduce-window.6
  11.2 3.4 %mul.59 = f32[128,2,2048]{2,1,0:T(2,128)} broadcast(bf16[128,2048]{1,0:T(8,128)(2,1)} %param.6), dimensions={0,2} | broadcast | bytes 2621440 | tf_op jit(solution)/shard_map/mul | solution.py:32
  14.6 3.7 %mul.60 = f32[256,2048]{1,0:T(8,128)} reshape(f32[128,2,2048]{2,1,0:T(2,128)} %mul.59) | data formatting | bytes 4194304 | tf_op jit(solution)/shard_map/mul | solution.py:32
  18.5 4.5 %scatter_custom_fusion = bf16[384,2048]{1,0:T(8,128)(2,1)} fusion(s32[256]{0:T(256)S(1)} %bitcast.41, f32[256,2048]{1,0:T(8,128)} %mul.60, f32[256]{0:T(256)S(1)} %mul.57, bf16[]{:T(256)} %constant.5.clone.1), kind=kCustom, calls=%fused_computation.12 | custom fusion | flops 1048576 | bytes 3671042 | tf_op jit(solution)/shard_map/scatter | solution.py:36
  23.0 3.7 %reshape.77 = bf16[64,6,2048]{2,1,0:T(8,128)(2,1)} reshape(bf16[384,2048]{1,0:T(8,128)(2,1)} %scatter_custom_fusion) | data formatting | bytes 3145728 | tf_op jit(solution)/shard_map/reshape | solution.py:37
  26.7 71.2 %all_to_all.10 = bf16[64,6,2048]{2,1,0:T(8,128)(2,1)} all-to-all(bf16[64,6,2048]{2,1,0:T(8,128)(2,1)} %reshape.77), channel_id=1, replica_groups=mesh['dp'=16,'ctx'=16,'tp'=4] {'ctx','tp'}, dimensions={0} | all-to-all | bytes 3145728 | tf_op jit(solution)/shard_map/all_to_all | solution.py:38
  97.9 3.7 %reshape.78 = bf16[384,2048]{1,0:T(8,128)(2,1)} reshape(bf16[64,6,2048]{2,1,0:T(8,128)(2,1)} %all_to_all.10) | data formatting | bytes 3145728 | tf_op jit(solution)/shard_map/reshape | solution.py:39
  101.7 5.0 %fusion.4 = bf16[768,2048]{0,1:T(8,128)(2,1)} fusion(bf16[384,2048]{1,0:T(8,128)(2,1)} %reshape.78, bf16[384,768]{1,0:T(8,128)(2,1)} %param.5), kind=kOutput, calls=%fused_computation.7 | convolution fusion | flops 1209532416 | bytes 5308416 | tf_op jit(solution)/shard_map/dot_general | solution.py:44
  106.7 4.7 %copy.24 = bf16[768,2048]{1,0:T(8,128)(2,1)} copy(bf16[768,2048]{0,1:T(8,128)(2,1)} %fusion.4) | data formatting | bytes 6291456
  111.5 3.6 %fusion.5 = bf16[384,2048]{1,0:T(8,128)(2,1)} fusion(bf16[384,768]{1,0:T(8,128)(2,1)} %param.5, bf16[1,768,2048]{2,1,0:T(8,128)(2,1)S(1)} %copy-done), kind=kOutput, calls=%fused_computation.8 | convolution fusion | flops 1208745984 | bytes 5308416 | tf_op jit(solution)/shard_map/dot_general | solution.py:26
  115.1 3.7 %reshape.74 = bf16[64,6,2048]{2,1,0:T(8,128)(2,1)} reshape(bf16[384,2048]{1,0:T(8,128)(2,1)} %fusion.5) | data formatting | bytes 3145728 | tf_op jit(solution)/shard_map/reshape | solution.py:27
  118.8 5.5 %all-to-all-start = ((bf16[64,6,2048]{2,1,0:T(8,128)(2,1)}), bf16[64,6,2048]{2,1,0:T(8,128)(2,1)}, u32[]{:S(2)}, u32[]{:S(2)}) async-start(bf16[64,6,2048]{2,1,0:T(8,128)(2,1)} %reshape.74), calls=%async_computation | async-start | bytes 4194304 | tf_op jit(solution)/shard_map/all_to_all | solution.py:28
  124.3 52.0 %all-to-all-done = bf16[64,6,2048]{2,1,0:T(8,128)(2,1)} async-done(((bf16[64,6,2048]{2,1,0:T(8,128)(2,1)}), bf16[64,6,2048]{2,1,0:T(8,128)(2,1)}, u32[]{:S(2)}, u32[]{:S(2)}) %all-to-all-start) | async-done | bytes 1572896 | tf_op jit(solution)/shard_map/all_to_all | solution.py:28
  176.3 3.8 %reshape.75 = bf16[384,2048]{1,0:T(8,128)(2,1)} reshape(bf16[64,6,2048]{2,1,0:T(8,128)(2,1)} %all-to-all-done) | data formatting | bytes 3145728 | tf_op jit(solution)/shard_map/reshape | solution.py:29
  180.1 5.0 %gather_fusion = bf16[256,2048]{1,0:T(8,128)(2,1)} fusion(bf16[384,2048]{1,0:T(8,128)(2,1)} %reshape.75, s32[1024]{0:T(1024)S(1)} %pad_clamp_fusion), kind=kCustom, calls=%fused_computation | custom fusion | bytes 2098176 | tf_op jit(solution)/shard_map/gather | solution.py:30
  185.1 3.3 %reshape.79 = f32[128,2,2048]{2,1,0:T(2,128)} reshape(bf16[256,2048]{1,0:T(8,128)(2,1)} %gather_fusion) | data formatting | bytes 3145728 | tf_op jit(solution)/shard_map/convert_element_type | solution.py:30
  188.4 5.7 %multiply_reduce_fusion = bf16[128,2048]{1,0:T(8,128)(2,1)} fusion(f32[128,2,2048]{2,1,0:T(2,128)} %reshape.79, f32[128,2]{1,0:T(8,128)S(1)} %copy.17), kind=kLoop, calls=%fused_computation.10 | loop fusion | flops 786432 | bytes 2622464 | tf_op jit(solution)/shard_map/reduce_sum | solution.py:31
  194.1 2.2 %fusion.8 = bf16[384,768]{1,0:T(8,128)(2,1)} fusion(bf16[384,2048]{1,0:T(8,128)(2,1)S(1)} %copy-done.1, bf16[1,768,2048]{2,1,0:T(8,128)(2,1)S(1)} %copy-done), kind=kOutput, calls=%fused_computation.11 | convolution fusion | flops 1208254464 | bytes 5308416 | tf_op jit(solution)/shard_map/dot_general | solution.py:40
  196.3 1.9 copy.25
  198.3 1.9 fusion.14
  200.2 1.9 copy.23
  (19 shorter events, 1.1 us)
Async XLA Ops:
  7.2 104.3 %copy-start = (bf16[1,768,2048]{2,1,0:T(8,128)(2,1)S(1)}, bf16[1,768,2048]{2,1,0:T(8,128)(2,1)}, u32[]{:S(2)}) copy-start(bf16[1,768,2048]{2,1,0:T(8,128)(2,1)} %param.9) | copy-start | bytes 9437188
  7.2 189.2 %reduce-scatter.4.cloned.1.call-start = ((), (), s32[]{:S(2)}) async-start(), calls=%async_computation.3 | async-start | bytes 3342336
  118.8 57.5 %all-to-all-start = ((bf16[64,6,2048]{2,1,0:T(8,128)(2,1)}), bf16[64,6,2048]{2,1,0:T(8,128)(2,1)}, u32[]{:S(2)}, u32[]{:S(2)}) async-start(bf16[64,6,2048]{2,1,0:T(8,128)(2,1)} %reshape.74), calls=%async_computation | async-start | bytes 4194304 | tf_op jit(solution)/shard_map/all_to_all | solution.py:28
  188.4 5.7 %copy-start.1 = (bf16[384,2048]{1,0:T(8,128)(2,1)S(1)}, bf16[384,2048]{1,0:T(8,128)(2,1)}, u32[]{:S(2)}) copy-start(bf16[384,2048]{1,0:T(8,128)(2,1)} %reshape.78) | copy-start | bytes 4718596
Sparse Core Ops, SparseCore 0:
  111.6 67.0 reduce-scatter.3
where the time goes:
time: 210 us; the launch traced here: 209 us
  blocking collectives  71.2 us (34%)
  waiting for transfers between devices  52.1 us (25%)
  local copies, waits for them, and re-layouts  41.4 us (20%)
  between operations  14.1 us (7%)
  other arithmetic  13.8 us (7%)
  matrix products  10.9 us (5%)
  starting transfers between devices  5.52 us (3%)
    all_to_all x1, blocking collectives, local(): lax.all_to_all(outgoing, ('ctx', 'tp'), split_axis=0, concat_axis=0, tile...  71.2 us
    all_to_all x1, waiting for transfers between devices, local(): lax.all_to_all(expert_out, ('ctx', 'tp'), split_axis=0, concat_axis=0, ti...  52 us
    unnamed x9, local copies, waits for them, and re-layouts  10.2 us
    mul x2, local copies, waits for them, and re-layouts, local(): gate_weights[:, :, None] * grad_output[:, None, :].astype(jnp.float32)  7.11 us
    reduce_sum x1, other arithmetic, local(): jnp.sum(gate_weights[:, :, None] * picked, axis=1).astype(jnp.bfloat16)  5.69 us
    all_to_all x1, starting transfers between devices, local(): lax.all_to_all(expert_out, ('ctx', 'tp'), split_axis=0, concat_axis=0, ti...  5.48 us
    dot_general x1, matrix products, local(): lax.dot_general(hidden, incoming, (((0,), (0,)), ((), ())), preferred_ele...  5.04 us
    gather x1, local copies, waits for them, and re-layouts, local(): returned[positions].astype(jnp.float32)  4.97 us
  transfers between devices with their start and end apart: 2, of which 1 were waited for; matrix products, arithmetic and copies ran while one was open for 13% of the time, Pallas kernels for 0%

commit v1 on v0

v1 whole, which is shorter than its diff:
```python
import functools

import jax
import jax.numpy as jnp
from jax import lax
from jax.experimental import pallas as pl
from jax.experimental.pallas import tpu as pltpu
from jax.sharding import PartitionSpec as P

MESH = pl.DeviceIdType.MESH
GRAD_SCALE = 0.015625
F32, BF16 = jnp.float32, jnp.bfloat16

NY, NX, NC, NZ = 8, 4, 2, 16
CAP = 6
GROUP = 8 * CAP
ROWS = 64 * CAP
CHUNKS = 4
HUB, PLANE_MEMBER, Z_MEMBER = 4, 0, 2


def events(chunks):
    tick = 34.0 / chunks
    out = []
    for k in range(chunks):
        out.append((0.0 + 0.01 * k, "send_y", k, 0))
        arrive_y = 4.0 + tick * (k + 1)
        out.append((arrive_y, "send_x", k, 0))
        arrive_x = arrive_y + 2.0 + tick * 0.55
        out.append((arrive_x, "part", k, 0))
        for j in range(1, 9):
            out.append((arrive_x + 2.6 * j, "ring", k, j))
        out.append((1.0 + tick * k * 0.8, "back_x", k, 0))
        out.append((4.0 + tick * (chunks - 1.1 + k), "back_y", k, 0))
        out.append((7.0 + tick * (chunks + 1 + k), "combine", k, 0))
    return sorted(out)


def kernel(
    ids_ref, gate_ref, hid_hbm, grad_hbm, w_hbm,
    comb_hbm, gh_hbm, gd_hbm,
    hid, grad, w, hp, hpt, perm, unsort, slot_pick, pick0, pick1, slot_gate, tok_gate,
    y_out, y_in, x_out, x_in, part, ring_up, ring_dn,
    ex, bx_in, by_out, by_in, gh_acc, comb, gh, gd,
    in_sem, out_sem, ring_ok, plane_ok, z_ok,
    y_s, y_r, x_s, x_r, bx_s, bx_r, by_s, by_r, up_s, up_r, dn_s, dn_r,
):
    tok = grad.shape[0]
    width = y_in.shape[2]
    z = lax.axis_index("dp")
    ctx = lax.axis_index("ctx")
    tp = lax.axis_index("tp")
    c = lax.rem(ctx, 2)
    x = lax.rem(ctx // 2, 4)
    y = tp * 2 + ctx // 8

    def dev(dz=0, dy=0, dx=0, dc=0):
        ny = lax.rem(y + (dy + NY), NY)
        nx = lax.rem(x + (dx + NX), NX)
        nc = lax.rem(c + (dc + NC), NC)
        nz = lax.rem(z + (dz + NZ), NZ)
        return {"dp": nz, "ctx": (lax.rem(ny, 2) * NX + nx) * NC + nc, "tp": ny // 2}

    loads = [
        pltpu.make_async_copy(grad_hbm, grad, in_sem.at[0]),
        pltpu.make_async_copy(hid_hbm, hid, in_sem.at[1]),
        pltpu.make_async_copy(w_hbm.at[0], w, in_sem.at[2]),
    ]
    for cp in loads:
        cp.start()

    barrier = pltpu.get_barrier_semaphore()

    def tell_ring(sem):
        for d in range(1, NY):
            pl.semaphore_signal(sem, inc=1, device_id=dev(dy=d), device_id_type=MESH)

    @pl.when(y != HUB)
    def _():
        pl.semaphore_signal(barrier, inc=1, device_id=dev(dy=HUB - y + NY), device_id_type=MESH)

    def greet_ring():
        @pl.when(y == HUB)
        def _():
            pl.semaphore_wait(barrier, NY - 1)
            tell_ring(ring_ok)

        @pl.when(y != HUB)
        def _():
            pl.semaphore_wait(ring_ok, 1)

        @pl.when(y == PLANE_MEMBER)
        def _():
            for d in range(1, 8):
                pl.semaphore_signal(barrier, inc=1, device_id=dev(dx=d // 2, dc=d % 2), device_id_type=MESH)

        @pl.when(y == Z_MEMBER)
        def _():
            for d in (1, -1):
                pl.semaphore_signal(barrier, inc=1, device_id=dev(dz=d), device_id_type=MESH)

    def greet_others(member, count, sem):
        @pl.when(y == member)
        def _():
            pl.semaphore_wait(barrier, count)
            tell_ring(sem)

        @pl.when(y != member)
        def _():
            pl.semaphore_wait(sem, 1)

    def send(src, dst, ssem, rsem, device):
        return pltpu.make_async_remote_copy(
            src_ref=src, dst_ref=dst, send_sem=ssem, recv_sem=rsem, device_id=device, device_id_type=MESH
        )

    def group(d):
        return pl.ds(d * GROUP, GROUP)

    def y_copy(k, d):
        return send(y_out.at[k, group(d)], y_in.at[k, group(d)], y_s.at[k, d], y_r.at[k, d], dev(dy=d))

    def x_copy(k, d):
        return send(
            x_out.at[k, group(d)], x_in.at[k, group(d)], x_s.at[k, d], x_r.at[k, d], dev(dx=d // 2, dc=d % 2)
        )

    def bx_copy(k, d):
        return send(
            ex.at[k, group(d)], bx_in.at[k, group(d)], bx_s.at[k, d], bx_r.at[k, d], dev(dx=-(d // 2), dc=d % 2)
        )

    def by_copy(k, d):
        return send(by_out.at[k, group(d)], by_in.at[k, group(d)], by_s.at[k, d], by_r.at[k, d], dev(dy=-d))

    def block(b):
        return pl.ds(pl.multiple_of(lax.rem(b + 2 * NZ, NZ) * 48, 16), 48)

    def up_copy(k, j):
        return send(part.at[k, block(z + 8 - j)], ring_up.at[k, j], up_s.at[k, j], up_r.at[k, j], dev(dz=1))

    def dn_copy(k, j):
        return send(part.at[k, block(z - 7 + j)], ring_dn.at[k, j], dn_s.at[k, j], dn_r.at[k, j], dev(dz=-1))

    def dot(a, b):
        return jnp.dot(a, b, preferred_element_type=F32)

    ids, gates = ids_ref[...], gate_ref[...]
    e_iota = lax.broadcasted_iota(jnp.int32, (128, tok), 0)
    hot = [(ids[k : k + 1] == e_iota).astype(F32) for k in range(2)]
    sq_row = lax.broadcasted_iota(jnp.int32, (tok, tok), 0)
    sq_col = lax.broadcasted_iota(jnp.int32, (tok, tok), 1)
    before = dot((hot[0] + hot[1]).astype(BF16), (sq_row < sq_col).astype(BF16))
    r_iota = lax.broadcasted_iota(jnp.int32, (ROWS, tok), 0)
    picks = []
    for k in range(2):
        e = ids[k : k + 1]
        rank = jnp.sum(hot[k] * before, axis=0, keepdims=True).astype(jnp.int32)
        ye = (e & 3) * 2 + ((e >> 5) & 1)
        dy = (ye - y) & 7
        dx = (((e >> 3) & 3) - x) & 3
        dc = (((e >> 2) & 1) - c) & 1
        place = dy * GROUP + (dx * 2 + dc) * CAP + rank
        picks.append((r_iota == place).astype(F32))
    slot_pick[...] = (picks[0] + picks[1]).astype(BF16)
    slot_gate[...] = jnp.sum(picks[0] * gates[0:1] + picks[1] * gates[1:2], axis=1, keepdims=True)
    loads[0].wait()

    def do_send_y(k):
        cols = pl.ds(k * width, width)
        rows = (dot(slot_pick[...], grad[:, cols]) * slot_gate[...]).astype(BF16)
        y_in[k, 0:GROUP] = rows[0:GROUP]
        y_out[k, GROUP:] = rows[GROUP:]
        if k == 0:
            greet_ring()
        for d in (4, 3, 5, 2, 6, 1, 7):
            y_copy(k, d).start()

    def prepare():
        def parts_of(r):
            hi = (r * 1366) >> 16
            rest = r - hi * GROUP
            lo = (rest * 10923) >> 16
            return hi, lo, rest - lo * CAP

        def hidden_row(r):
            dxc, dy, i = parts_of(r)
            sy = (y - dy) & 7
            sx = (x - (dxc >> 1)) & 3
            sc = (c - (dxc & 1)) & 1
            return ((((sy & 1) * NX + sx) * NC + sc) * 4 + (sy >> 1)) * CAP + i

        for k, pick in enumerate((pick0, pick1)):
            pick[...] = jnp.transpose(picks[k]).astype(BF16)
            diagonal = jnp.where(sq_row == sq_col, gates[k : k + 1], 0.0)
            tok_gate[:, k : k + 1] = jnp.sum(diagonal, axis=1, keepdims=True)
        row = lax.broadcasted_iota(jnp.int32, (ROWS, 1), 0)
        col = lax.broadcasted_iota(jnp.int32, (1, ROWS), 1)
        hi, lo, i = parts_of(row)
        wide = lax.broadcasted_iota(jnp.int32, (ROWS, ROWS), 1)
        tall = lax.broadcasted_iota(jnp.int32, (ROWS, ROWS), 0)
        perm[...] = (wide == lo * GROUP + hi * CAP + i).astype(F32).astype(BF16)
        sort = (wide == hidden_row(row)).astype(F32).astype(BF16)
        unsort[...] = (tall == hidden_row(col)).astype(F32).astype(BF16)
        loads[1].wait()
        ordered = dot(sort, hid[...])
        hp[...] = ordered.astype(BF16)
        hpt[...] = jnp.transpose(ordered).astype(BF16)
        gh_acc[...] = jnp.zeros_like(gh_acc)
        loads[2].wait()

    def do_send_x(k):
        for d in range(1, NY):
            y_copy(k, d).wait_recv()
        rows = dot(perm[...], y_in[k]).astype(BF16)
        x_in[k, 0:GROUP] = rows[0:GROUP]
        x_out[k, GROUP:] = rows[GROUP:]
        for d in range(7, 0, -1):
            x_copy(k, d).start()

    def do_part(k):
        cols = pl.ds(k * width, width)
        for d in range(1, 8):
            x_copy(k, d).wait_recv()
        rows = x_in[k]
        part[k] = dot(hpt[...], rows).astype(BF16)
        up_copy(k, 0).start()
        dn_copy(k, 0).start()
        gh_acc[...] += lax.dot_general(rows, w[:, cols], (((1,), (1,)), ((), ())), preferred_element_type=F32)

    def do_ring(k, j):
        if j < 8:
            up_copy(k, j - 1).wait_recv()
            b = block(z + 8 - j)
            part[k, b] = (part[k, b].astype(F32) + ring_up[k, j - 1].astype(F32)).astype(BF16)
            up_copy(k, j).start()
            if j < 7:
                dn_copy(k, j - 1).wait_recv()
                b = block(z - 7 + j)
                part[k, b] = (part[k, b].astype(F32) + ring_dn[k, j - 1].astype(F32)).astype(BF16)
                dn_copy(k, j).start()
        else:
            up_copy(k, 7).wait_recv()
            dn_copy(k, 6).wait_recv()
            total = part[k, block(z)].astype(F32) + ring_up[k, 7].astype(F32) + ring_dn[k, 6].astype(F32)
            gd[:, pl.ds(k * width, width)] = (total * GRAD_SCALE).astype(BF16)

    def do_back_x(k):
        rows = dot(hp[...], w[:, pl.ds(k * width, width)]).astype(BF16)
        bx_in[k, 0:GROUP] = rows[0:GROUP]
        ex[k, GROUP:] = rows[GROUP:]
        for d in range(7, 0, -1):
            bx_copy(k, d).start()

    def do_back_y(k):
        for d in range(1, 8):
            bx_copy(k, d).wait_recv()
        rows = dot(perm[...], bx_in[k]).astype(BF16)
        by_in[k, 0:GROUP] = rows[0:GROUP]
        by_out[k, GROUP:] = rows[GROUP:]
        for d in (4, 3, 5, 2, 6, 1, 7):
            by_copy(k, d).start()

    def comb_store(k):
        cols = pl.ds(k * width, width)
        return pltpu.make_async_copy(comb.at[:, cols], comb_hbm.at[:, cols], out_sem.at[k])

    def do_combine(k):
        for d in range(1, NY):
            by_copy(k, d).wait_recv()
        rows = by_in[k]
        g = tok_gate[...]
        total = g[:, 0:1] * dot(pick0[...], rows) + g[:, 1:2] * dot(pick1[...], rows)
        comb[:, pl.ds(k * width, width)] = total.astype(BF16)
        comb_store(k).start()

    gh_store = pltpu.make_async_copy(gh, gh_hbm, out_sem.at[CHUNKS])
    gd_store = pltpu.make_async_copy(gd, gd_hbm, out_sem.at[CHUNKS + 1])
    prepared, joined, met_z, rings = False, False, False, 0
    for _, what, k, j in events(CHUNKS):
        if what == "send_y":
            do_send_y(k)
        else:
            if not prepared:
                prepare()
                prepared = True
            if not joined:
                greet_others(PLANE_MEMBER, 7, plane_ok)
                joined = True
            if what == "part" and not met_z:
                greet_others(Z_MEMBER, 2, z_ok)
                met_z = True
            if what == "send_x":
                do_send_x(k)
            elif what == "part":
                do_part(k)
                if k == CHUNKS - 1:
                    gh[...] = dot(unsort[...], gh_acc[...].astype(BF16)).astype(BF16)
                    gh_store.start()
            elif what == "ring":
                do_ring(k, j)
                if j == 8:
                    rings += 1
                    if rings == CHUNKS:
                        gd_store.start()
            elif what == "back_x":
                do_back_x(k)
            elif what == "back_y":
                do_back_y(k)
            else:
                do_combine(k)

    for k in range(CHUNKS):
        for d in range(1, 8):
            y_copy(k, d).wait_send()
            x_copy(k, d).wait_send()
            bx_copy(k, d).wait_send()
            by_copy(k, d).wait_send()
        for j in range(8):
            up_copy(k, j).wait_send()
        for j in range(7):
            dn_copy(k, j).wait_send()
        comb_store(k).wait()
    gh_store.wait()
    gd_store.wait()


def settle(a_ref, b_ref, c_ref, a_out, b_out, c_out, sem):
    copies = [
        pltpu.make_async_copy(src, dst, sem.at[i])
        for i, (src, dst) in enumerate(((a_ref, a_out), (b_ref, b_out), (c_ref, c_out)))
    ]
    for cp in copies:
        cp.start()
    for cp in copies:
        cp.wait()


def local(hidden, grad_output, expert_ids, gate_weights, w_down):
    rows, ff = hidden.shape
    tok, model = grad_output.shape
    width = model // CHUNKS
    any_spec = pl.BlockSpec(memory_space=pl.ANY)
    vmem_spec = pl.BlockSpec(memory_space=pltpu.VMEM)
    dma, regular = pltpu.SemaphoreType.DMA, pltpu.SemaphoreType.REGULAR
    chunked = pltpu.VMEM((CHUNKS, rows, width), BF16)
    combined, grad_hidden, grad_down = pl.pallas_call(
        kernel,
        out_shape=(
            jax.ShapeDtypeStruct((tok, model), BF16),
            jax.ShapeDtypeStruct((rows, ff), BF16),
            jax.ShapeDtypeStruct((ff // NZ, model), BF16),
        ),
        in_specs=[vmem_spec, vmem_spec, any_spec, any_spec, any_spec],
        out_specs=(any_spec, any_spec, any_spec),
        scratch_shapes=[
            pltpu.VMEM((rows, ff), BF16),
            pltpu.VMEM((tok, model), BF16),
            pltpu.VMEM((ff, model), BF16),
            pltpu.VMEM((rows, ff), BF16),
            pltpu.VMEM((ff, rows), BF16),
            pltpu.VMEM((rows, rows), BF16),
            pltpu.VMEM((rows, rows), BF16),
            pltpu.VMEM((rows, tok), BF16),
            pltpu.VMEM((tok, rows), BF16),
            pltpu.VMEM((tok, rows), BF16),
            pltpu.VMEM((rows, 1), F32),
            pltpu.VMEM((tok, 2), F32),
            chunked, chunked, chunked, chunked,
            pltpu.VMEM((CHUNKS, ff, width), BF16),
            pltpu.VMEM((CHUNKS, 8, ff // NZ, width), BF16),
            pltpu.VMEM((CHUNKS, 7, ff // NZ, width), BF16),
            chunked, chunked, chunked, chunked,
            pltpu.VMEM((rows, ff), F32),
            pltpu.VMEM((tok, model), BF16),
            pltpu.VMEM((rows, ff), BF16),
            pltpu.VMEM((ff // NZ, model), BF16),
            dma((3,)),
            dma((CHUNKS + 2,)),
            regular, regular, regular,
        ]
        + [dma((CHUNKS, 8))] * 12,
        compiler_params=pltpu.CompilerParams(
            collective_id=0, has_side_effects=True, vmem_limit_bytes=56 * 2**20
        ),
        name="moe_down",
    )(expert_ids.T, gate_weights.T, hidden, grad_output, w_down)
    combined, grad_hidden, grad_down = pl.pallas_call(
        settle,
        out_shape=(
            jax.ShapeDtypeStruct(combined.shape, BF16),
            jax.ShapeDtypeStruct(grad_hidden.shape, BF16),
            jax.ShapeDtypeStruct(grad_down.shape, BF16),
        ),
        in_specs=[any_spec] * 3,
        out_specs=(any_spec,) * 3,
        scratch_shapes=[dma((3,))],
        name="settle",
    )(combined, grad_hidden, grad_down)
    return combined, grad_hidden, grad_down[None]


def solution(mesh):
    return jax.shard_map(
        local,
        mesh=mesh,
        in_specs=(
            P(("dp", "ctx", "tp"), None),
            P(("dp", "ctx", "tp"), None),
            P(("dp", "ctx", "tp"), None),
            P(("dp", "ctx", "tp"), None),
            P(("ctx", "tp"), None, None),
        ),
        out_specs=(
            P(("dp", "ctx", "tp"), None),
            P(("dp", "ctx", "tp"), None),
            P(("ctx", "tp"), "dp", None),
        ),
        check_vma=False,
    )
```

time: 210 us -> 153 us (0.73)
  the two profiles are of different devices: /device:TPU:1 before, /device:TPU:6 now
where the time goes in v1:
time: 153 us; the launch traced here: 151 us
  Pallas kernels  150 us (98%)
    pallas_call x1, Pallas kernels, local(): pl.pallas_call(kernel, out_shape=(jax.ShapeDtypeStruct((tok, model), BF16...  110 us
    pallas_call x1, Pallas kernels, local(): pl.pallas_call(settle, out_shape=(jax.ShapeDtypeStruct(combined.shape, BF...  40.8 us

profile of v1, /device:TPU:6, one launch (start us, length us, event | category | flops | bytes accessed | tf_op | source)
XLA Modules:
  0.0 151.1 jit_solution(9812422087296944660)
XLA Ops:
  0.6 109.7 %moe_down.1 = (bf16[128,2048]{1,0:T(8,128)(2,1)}, bf16[384,768]{1,0:T(8,128)(2,1)}, bf16[48,2048]{1,0:T(8,128)(2,1)}) custom-call(s32[2,128]{1,0:T(2,128)} %bitcast.3, f32[2,128]{1,0:T(2,128)} %bitcast.4, bf16[384,768]{1,0:T(8,128)(2,1)} %hid_hbm.1, bf16[128,2048]{1,0:T(8,128)(2,1)} %grad_hbm.1, bf16[1,768,2048]{2,1,0:T(8,128)(2,1)} %w_hbm.1), custom_call_target="tpu_custom_call" | custom-call | tf_op jit(solution)/shard_map/moe_down/pallas_call | solution.py:347
  110.3 40.8 %settle.1 = (bf16[128,2048]{1,0:T(8,128)(2,1)}, bf16[384,768]{1,0:T(8,128)(2,1)}, bf16[48,2048]{1,0:T(8,128)(2,1)}) custom-call(bf16[128,2048]{1,0:T(8,128)(2,1)} %get-tuple-element.9.a_ref, bf16[384,768]{1,0:T(8,128)(2,1)} %get-tuple-element.10.b_ref, bf16[48,2048]{1,0:T(8,128)(2,1)} %get-tuple-element.11.c_ref), custom_call_target="tpu_custom_call" | custom-call | tf_op jit(solution)/shard_map/settle/pallas_call | solution.py:388

commit v2 on v1

v2 whole, which is shorter than its diff:
```python
import functools

import jax
import jax.numpy as jnp
from jax import lax
from jax.experimental import pallas as pl
from jax.experimental.pallas import tpu as pltpu
from jax.sharding import PartitionSpec as P

MESH = pl.DeviceIdType.MESH
GRAD_SCALE = 0.015625
F32, BF16 = jnp.float32, jnp.bfloat16

NY, NX, NC, NZ = 8, 4, 2, 16
CAP = 6
GROUP = 8 * CAP
ROWS = 64 * CAP
HUB, PLANE_MEMBER, Z_MEMBER = 4, 0, 2
UNITS, WIDTH = 8, 256
CHUNKS = ((0, 2), (2, 2), (4, 2), (6, 1), (7, 1))
LAST = len(CHUNKS) - 1
IN_FLIGHT = 5
STRIDES = (1, 1, 1, 1, 2)
REACH = max(STRIDES)


def ring_steps(k):
    return -(-8 // STRIDES[k])


def events():
    out = []
    y_end = [13.5, 22.0, 30.6, 35.0, 39.0]
    part_at = [19.5, 28.0, 36.5, 40.0, 43.5]
    back_x_at = [6.0, 7.0, 23.5, 32.0, 42.0]
    back_y_at = [18.5, 33.0, 42.0, 50.0, 54.0]
    for k in range(len(CHUNKS)):
        out.append((0.1 * k, "send_y", k, 0))
        out.append((back_x_at[k], "back_x", k, 0))
        out.append((y_end[k], "send_x", k, 0))
        out.append((back_y_at[k], "back_y", k, 0))
        out.append((part_at[k], "part", k, 0))
        for j in range(1, ring_steps(k) + 1):
            out.append((part_at[k] + (3.0 if STRIDES[k] == 1 else 3.5) * j, "ring", k, j))
        out.append((66.0 + k, "combine", k, 0))
    return sorted(out)


def kernel(
    ids_ref, gate_ref, hid_hbm, grad_hbm, w_hbm,
    comb_hbm, gh_hbm, gd_hbm,
    hid, grad, w, hp, hpt, perm, unsort, slot_pick, pick0, pick1, slot_gate, tok_gate,
    y_out, y_in, x_out, x_in, part, ring_in,
    ex, bx_in, by_out, by_in, gh_acc, comb, gh, gd,
    in_sem, out_sem, ring_ok, plane_ok, z_ok,
    y_s, y_r, x_s, x_r, bx_s, bx_r, by_s, by_r, ring_s, ring_r,
):
    tok = grad.shape[0]
    z = lax.axis_index("dp")
    ctx = lax.axis_index("ctx")
    tp = lax.axis_index("tp")
    c = lax.rem(ctx, 2)
    x = lax.rem(ctx // 2, 4)
    y = tp * 2 + ctx // 8

    def dev(dz=0, dy=0, dx=0, dc=0):
        ny = lax.rem(y + (dy + NY), NY)
        nx = lax.rem(x + (dx + NX), NX)
        nc = lax.rem(c + (dc + NC), NC)
        nz = lax.rem(z + (dz + NZ), NZ)
        return {"dp": nz, "ctx": (lax.rem(ny, 2) * NX + nx) * NC + nc, "tp": ny // 2}

    loads = [
        pltpu.make_async_copy(grad_hbm, grad, in_sem.at[0]),
        pltpu.make_async_copy(hid_hbm, hid, in_sem.at[1]),
        pltpu.make_async_copy(w_hbm.at[0], w, in_sem.at[2]),
    ]
    loads[0].start()

    barrier = pltpu.get_barrier_semaphore()

    def tell_ring(sem):
        for d in range(1, NY):
            pl.semaphore_signal(sem, inc=1, device_id=dev(dy=d), device_id_type=MESH)

    @pl.when(y != HUB)
    def _():
        pl.semaphore_signal(barrier, inc=1, device_id=dev(dy=HUB - y + NY), device_id_type=MESH)

    def greet_ring():
        @pl.when(y == HUB)
        def _():
            pl.semaphore_wait(barrier, NY - 1)
            tell_ring(ring_ok)

        @pl.when(y != HUB)
        def _():
            pl.semaphore_wait(ring_ok, 1)

        @pl.when(y == PLANE_MEMBER)
        def _():
            for d in range(1, 8):
                pl.semaphore_signal(barrier, inc=1, device_id=dev(dx=d // 2, dc=d % 2), device_id_type=MESH)

        @pl.when(y == Z_MEMBER)
        def _():
            for d in [sign * hop for hop in range(1, REACH + 1) for sign in (1, -1)]:
                pl.semaphore_signal(barrier, inc=1, device_id=dev(dz=d), device_id_type=MESH)

    def greet_others(member, count, sem):
        @pl.when(y == member)
        def _():
            pl.semaphore_wait(barrier, count)
            tell_ring(sem)

        @pl.when(y != member)
        def _():
            pl.semaphore_wait(sem, 1)

    def send(src, dst, ssem, rsem, device):
        return pltpu.make_async_remote_copy(
            src_ref=src, dst_ref=dst, send_sem=ssem, recv_sem=rsem, device_id=device, device_id_type=MESH
        )

    def group(d):
        return pl.ds(d * GROUP, GROUP)

    def units(k):
        return pl.ds(CHUNKS[k][0], CHUNKS[k][1])

    def columns(k):
        return pl.ds(CHUNKS[k][0] * WIDTH, CHUNKS[k][1] * WIDTH)

    def each_unit(k):
        return [(u, pl.ds(u * WIDTH, WIDTH)) for u in range(CHUNKS[k][0], CHUNKS[k][0] + CHUNKS[k][1])]

    def message(out, into, sems, k, d, device):
        at = (units(k), group(d))
        return send(out.at[at], into.at[at], sems[0].at[k, d], sems[1].at[k, d], device)

    def y_copy(k, d):
        return message(y_out, y_in, (y_s, y_r), k, d, dev(dy=d))

    def x_copy(k, d):
        return message(x_out, x_in, (x_s, x_r), k, d, dev(dx=d // 2, dc=d % 2))

    def bx_copy(k, d):
        return message(ex, bx_in, (bx_s, bx_r), k, d, dev(dx=-(d // 2), dc=d % 2))

    def by_copy(k, d):
        return message(by_out, by_in, (by_s, by_r), k, d, dev(dy=-d))

    def split(rows, u, own, out):
        rows = rows.astype(BF16)
        own[u, 0:GROUP] = rows[0:GROUP]
        out[u, GROUP:] = rows[GROUP:]

    def block(b):
        return pl.ds(pl.multiple_of(lax.rem(b + 2 * NZ, NZ) * 48, 16), 48)

    def distances(k, way, j):
        far, stride = 8 if way == k % 2 else 7, STRIDES[k]
        return [d for d in range(far - stride * j, far - stride * (j + 1), -1) if d >= 1]

    def ring_block(way, d):
        return block(z + d if way == 0 else z - d)

    def ring_copy(k, way, d):
        hop = min(STRIDES[k], d)
        return send(
            part.at[units(k), ring_block(way, d)],
            ring_in.at[way, d - 1, units(k)],
            ring_s.at[way, k, d - 1],
            ring_r.at[way, k, d - 1],
            dev(dz=hop if way == 0 else -hop),
        )

    def dot(a, b):
        return jnp.dot(a, b, preferred_element_type=F32)

    ids, gates = ids_ref[...], gate_ref[...]
    e_iota = lax.broadcasted_iota(jnp.int32, (128, tok), 0)
    hot = [(ids[k : k + 1] == e_iota).astype(F32) for k in range(2)]
    sq_row = lax.broadcasted_iota(jnp.int32, (tok, tok), 0)
    sq_col = lax.broadcasted_iota(jnp.int32, (tok, tok), 1)
    before = dot((hot[0] + hot[1]).astype(BF16), (sq_row < sq_col).astype(BF16))
    r_iota = lax.broadcasted_iota(jnp.int32, (ROWS, tok), 0)
    picks = []
    for k in range(2):
        e = ids[k : k + 1]
        rank = jnp.sum(hot[k] * before, axis=0, keepdims=True).astype(jnp.int32)
        ye = (e & 3) * 2 + ((e >> 5) & 1)
        dy = (ye - y) & 7
        dx = (((e >> 3) & 3) - x) & 3
        dc = (((e >> 2) & 1) - c) & 1
        place = dy * GROUP + (dx * 2 + dc) * CAP + rank
        picks.append((r_iota == place).astype(F32))
    slot_pick[...] = (picks[0] + picks[1]).astype(BF16)
    slot_gate[...] = jnp.sum(picks[0] * gates[0:1] + picks[1] * gates[1:2], axis=1, keepdims=True)
    loads[0].wait()
    loads[1].start()
    loads[2].start()

    far_first = (4, 3, 5, 2, 6, 1, 7)

    def do_send_y(k):
        for u, cols in each_unit(k):
            split(dot(slot_pick[...], grad[:, cols]) * slot_gate[...], u, y_in, y_out)
        if k == 0:
            greet_ring()
        for d in far_first:
            y_copy(k, d).start()

    def prepare():
        def parts_of(r):
            hi = (r * 1366) >> 16
            rest = r - hi * GROUP
            lo = (rest * 10923) >> 16
            return hi, lo, rest - lo * CAP

        def hidden_row(r):
            dxc, dy, i = parts_of(r)
            sy = (y - dy) & 7
            sx = (x - (dxc >> 1)) & 3
            sc = (c - (dxc & 1)) & 1
            return ((((sy & 1) * NX + sx) * NC + sc) * 4 + (sy >> 1)) * CAP + i

        for k, pick in enumerate((pick0, pick1)):
            pick[...] = jnp.transpose(picks[k]).astype(BF16)
            diagonal = jnp.where(sq_row == sq_col, gates[k : k + 1], 0.0)
            tok_gate[:, k : k + 1] = jnp.sum(diagonal, axis=1, keepdims=True)
        row = lax.broadcasted_iota(jnp.int32, (ROWS, 1), 0)
        col = lax.broadcasted_iota(jnp.int32, (1, ROWS), 1)
        hi, lo, i = parts_of(row)
        wide = lax.broadcasted_iota(jnp.int32, (ROWS, ROWS), 1)
        tall = lax.broadcasted_iota(jnp.int32, (ROWS, ROWS), 0)
        perm[...] = (wide == lo * GROUP + hi * CAP + i).astype(F32).astype(BF16)
        sort = (wide == hidden_row(row)).astype(F32).astype(BF16)
        unsort[...] = (tall == hidden_row(col)).astype(F32).astype(BF16)
        loads[1].wait()
        ordered = dot(sort, hid[...])
        hp[...] = ordered.astype(BF16)
        hpt[...] = jnp.transpose(ordered).astype(BF16)
        gh_acc[...] = jnp.zeros_like(gh_acc)
        loads[2].wait()

    def arrived_y(k):
        for d in range(1, NY):
            y_copy(k, d).wait_recv()

    def do_send_x(k):
        for u, _ in each_unit(k):
            split(dot(perm[...], y_in[u]), u, x_in, x_out)
        for d in range(7, 0, -1):
            x_copy(k, d).start()

    def do_part(k):
        for d in range(1, 8):
            x_copy(k, d).wait_recv()
        for u, _ in each_unit(k):
            part[u] = dot(hpt[...], x_in[u]).astype(BF16)
        for way in range(2):
            for d in distances(k, way, 0):
                ring_copy(k, way, d).start()
        for u, cols in each_unit(k):
            gh_acc[...] += lax.dot_general(
                x_in[u], w[:, cols], (((1,), (1,)), ((), ())), preferred_element_type=F32
            )

    def do_ring(k, j):
        stride = STRIDES[k]
        for way in range(2):
            for d in distances(k, way, j):
                ring_copy(k, way, d + stride).wait_recv()
                at = (units(k), ring_block(way, d))
                part[at] = (part[at].astype(F32) + ring_in[way, d + stride - 1, units(k)].astype(F32)).astype(BF16)
                ring_copy(k, way, d).start()
        if j == ring_steps(k):
            ends = [(way, d) for way in range(2) for d in range(1, stride + 1)]
            for way, d in ends:
                ring_copy(k, way, d).wait_recv()
            for u, cols in each_unit(k):
                total = part[u, block(z)].astype(F32)
                for way, d in ends:
                    total += ring_in[way, d - 1, u].astype(F32)
                gd[:, cols] = (total * GRAD_SCALE).astype(BF16)

    def do_back_x(k):
        for u, cols in each_unit(k):
            split(dot(hp[...], w[:, cols]), u, bx_in, ex)
        for d in range(7, 0, -1):
            bx_copy(k, d).start()

    def do_back_y(k):
        for d in range(1, 8):
            bx_copy(k, d).wait_recv()
        for u, _ in each_unit(k):
            split(dot(perm[...], bx_in[u]), u, by_in, by_out)
        for d in far_first:
            by_copy(k, d).start()

    def comb_store(k):
        cols = columns(k)
        return pltpu.make_async_copy(comb.at[:, cols], comb_hbm.at[:, cols], out_sem.at[k])

    def arrived_back(k):
        for d in range(1, NY):
            by_copy(k, d).wait_recv()

    def do_combine(k):
        g = tok_gate[...]
        for u, cols in each_unit(k):
            total = g[:, 0:1] * dot(pick0[...], by_in[u]) + g[:, 1:2] * dot(pick1[...], by_in[u])
            comb[:, cols] = total.astype(BF16)
        comb_store(k).start()

    gh_store = pltpu.make_async_copy(gh, gh_hbm, out_sem.at[LAST + 1])
    gd_store = pltpu.make_async_copy(gd, gd_hbm, out_sem.at[LAST + 2])
    prepared, joined, met_z, rings, came, came_back = False, False, False, 0, -1, -1
    for _, what, k, j in events():
        if what == "send_y":
            if k >= IN_FLIGHT:
                came = k - IN_FLIGHT
                arrived_y(came)
            do_send_y(k)
            continue
        if not prepared:
            prepare()
            prepared = True
        if not joined:
            greet_others(PLANE_MEMBER, 7, plane_ok)
            joined = True
        if what == "part" and not met_z:
            greet_others(Z_MEMBER, 2 * REACH, z_ok)
            met_z = True
        if what == "send_x":
            if came < k:
                came = k
                arrived_y(k)
            do_send_x(k)
        elif what == "part":
            do_part(k)
            if k == LAST:
                gh[...] = dot(unsort[...], gh_acc[...].astype(BF16)).astype(BF16)
                gh_store.start()
        elif what == "ring":
            do_ring(k, j)
            if j == ring_steps(k):
                rings += 1
                if rings > LAST:
                    gd_store.start()
        elif what == "back_x":
            do_back_x(k)
        elif what == "back_y":
            do_back_y(k)
        else:
            arrived_back(k)
            do_combine(k)

    for k in range(LAST + 1):
        for d in range(1, 8):
            y_copy(k, d).wait_send()
            x_copy(k, d).wait_send()
            bx_copy(k, d).wait_send()
            by_copy(k, d).wait_send()
        for way in range(2):
            for j in range(ring_steps(k)):
                for d in distances(k, way, j):
                    ring_copy(k, way, d).wait_send()
        comb_store(k).wait()
    gh_store.wait()
    gd_store.wait()


def settle(*refs):
    for src, dst in zip(refs[:3], refs[3:]):
        dst[...] = src[...]


def local(hidden, grad_output, expert_ids, gate_weights, w_down):
    rows, ff = hidden.shape
    tok, model = grad_output.shape
    any_spec = pl.BlockSpec(memory_space=pl.ANY)
    vmem_spec = pl.BlockSpec(memory_space=pltpu.VMEM)
    dma, regular = pltpu.SemaphoreType.DMA, pltpu.SemaphoreType.REGULAR
    chunked = pltpu.VMEM((UNITS, rows, WIDTH), BF16)
    combined, grad_hidden, grad_down = pl.pallas_call(
        kernel,
        out_shape=(
            jax.ShapeDtypeStruct((tok, model), BF16),
            jax.ShapeDtypeStruct((rows, ff), BF16),
            jax.ShapeDtypeStruct((ff // NZ, model), BF16),
        ),
        in_specs=[vmem_spec, vmem_spec, any_spec, any_spec, any_spec],
        out_specs=(any_spec, any_spec, any_spec),
        scratch_shapes=[
            pltpu.VMEM((rows, ff), BF16),
            pltpu.VMEM((tok, model), BF16),
            pltpu.VMEM((ff, model), BF16),
            pltpu.VMEM((rows, ff), BF16),
            pltpu.VMEM((ff, rows), BF16),
            pltpu.VMEM((rows, rows), BF16),
            pltpu.VMEM((rows, rows), BF16),
            pltpu.VMEM((rows, tok), BF16),
            pltpu.VMEM((tok, rows), BF16),
            pltpu.VMEM((tok, rows), BF16),
            pltpu.VMEM((rows, 1), F32),
            pltpu.VMEM((tok, 2), F32),
            chunked, chunked, chunked, chunked,
            pltpu.VMEM((UNITS, ff, WIDTH), BF16),
            pltpu.VMEM((2, 8, UNITS, ff // NZ, WIDTH), BF16),
            chunked, chunked, chunked, chunked,
            pltpu.VMEM((rows, ff), F32),
            pltpu.VMEM((tok, model), BF16),
            pltpu.VMEM((rows, ff), BF16),
            pltpu.VMEM((ff // NZ, model), BF16),
            dma((3,)),
            dma((LAST + 3,)),
            regular, regular, regular,
        ]
        + [dma((LAST + 1, 8))] * 8
        + [dma((2, LAST + 1, 8))] * 2,
        compiler_params=pltpu.CompilerParams(
            collective_id=0, has_side_effects=True, vmem_limit_bytes=56 * 2**20
        ),
        name="moe_down",
    )(expert_ids.T, gate_weights.T, hidden, grad_output, w_down)
    combined, grad_hidden, grad_down = pl.pallas_call(
        settle,
        out_shape=(
            jax.ShapeDtypeStruct(combined.shape, BF16),
            jax.ShapeDtypeStruct(grad_hidden.shape, BF16),
            jax.ShapeDtypeStruct(grad_down.shape, BF16),
        ),
        in_specs=[vmem_spec] * 3,
        out_specs=(vmem_spec,) * 3,
        name="settle",
    )(combined, grad_hidden, grad_down)
    return combined, grad_hidden, grad_down[None]


def solution(mesh):
    return jax.shard_map(
        local,
        mesh=mesh,
        in_specs=(
            P(("dp", "ctx", "tp"), None),
            P(("dp", "ctx", "tp"), None),
            P(("dp", "ctx", "tp"), None),
            P(("dp", "ctx", "tp"), None),
            P(("ctx", "tp"), None, None),
        ),
        out_specs=(
            P(("dp", "ctx", "tp"), None),
            P(("dp", "ctx", "tp"), None),
            P(("ctx", "tp"), "dp", None),
        ),
        check_vma=False,
    )
```

time: 153 us -> 107 us (0.70)
  Pallas kernels: 150 us -> 105 us
    pallas_call x1, Pallas kernels: 40.8 us -> 2.35 us  [local(): pl.pallas_call(settle, out_shape=(jax.ShapeDtypeStruct(combined.shape, BF...]
    pallas_call x1, Pallas kernels: 110 us -> 103 us  [local(): pl.pallas_call(kernel, out_shape=(jax.ShapeDtypeStruct((tok, model), BF16...]
where the time goes in v2:
time: 107 us; the launch traced here: 106 us
  Pallas kernels  105 us (98%)
    pallas_call x1, Pallas kernels, local(): pl.pallas_call(kernel, out_shape=(jax.ShapeDtypeStruct((tok, model), BF16...  103 us
    pallas_call x1, Pallas kernels, local(): pl.pallas_call(settle, out_shape=(jax.ShapeDtypeStruct(combined.shape, BF...  2.35 us

profile of v2, /device:TPU:6, one launch (start us, length us, event | category | flops | bytes accessed | tf_op | source)
XLA Modules:
  0.0 105.7 jit_solution(18135502483806462083)
XLA Ops:
  0.6 102.7 %moe_down.1 = (bf16[128,2048]{1,0:T(8,128)(2,1)}, bf16[384,768]{1,0:T(8,128)(2,1)}, bf16[48,2048]{1,0:T(8,128)(2,1)}) custom-call(s32[2,128]{1,0:T(2,128)} %bitcast.3, f32[2,128]{1,0:T(2,128)} %bitcast.4, bf16[384,768]{1,0:T(8,128)(2,1)} %hid_hbm.1, bf16[128,2048]{1,0:T(8,128)(2,1)} %grad_hbm.1, bf16[1,768,2048]{2,1,0:T(8,128)(2,1)} %w_hbm.1), custom_call_target="tpu_custom_call" | custom-call | tf_op jit(solution)/shard_map/moe_down/pallas_call | solution.py:387
  103.4 2.3 %settle.1 = (bf16[128,2048]{1,0:T(8,128)(2,1)}, bf16[384,768]{1,0:T(8,128)(2,1)}, bf16[48,2048]{1,0:T(8,128)(2,1)}) custom-call(bf16[128,2048]{1,0:T(8,128)(2,1)} %get-tuple-element.9.refs_0_, bf16[384,768]{1,0:T(8,128)(2,1)} %get-tuple-element.10.refs_1_, bf16[48,2048]{1,0:T(8,128)(2,1)} %get-tuple-element.11.refs_2_), custom_call_target="tpu_custom_call" | custom-call | tf_op jit(solution)/shard_map/settle/pallas_call | solution.py:428

commit v3 on v2

--- a/solution.py
+++ b/solution.py
@@ -30,10 +30,13 @@
 
 def events():
     out = []
-    y_end = [13.5, 22.0, 30.6, 35.0, 39.0]
-    part_at = [19.5, 28.0, 36.5, 40.0, 43.5]
-    back_x_at = [6.0, 7.0, 23.5, 32.0, 42.0]
-    back_y_at = [18.5, 33.0, 42.0, 50.0, 54.0]
+    y_end = [7.42, 13.14, 17.44, 25.57, 30.53]
+    part_at = [25.57, 28.87, 36.37, 39.58, 43.37]
+    ring_at = [25.57, 30.08, 36.37, 39.58, 49.04]
+    ring_step = [3.0, 3.03, 3.4, 2.99, 3.45]
+    back_x_at = [3.82, 5.21, 27.02, 33.99, 42.09]
+    back_y_at = [15.32, 18.17, 47.28, 49.1, 55.19]
+    combine_at = [57.75, 60.52, 62.63, 70.92, 96.62]
     for k in range(len(CHUNKS)):
         out.append((0.1 * k, "send_y", k, 0))
         out.append((back_x_at[k], "back_x", k, 0))
@@ -41,8 +44,8 @@
         out.append((back_y_at[k], "back_y", k, 0))
         out.append((part_at[k], "part", k, 0))
         for j in range(1, ring_steps(k) + 1):
-            out.append((part_at[k] + (3.0 if STRIDES[k] == 1 else 3.5) * j, "ring", k, j))
-        out.append((66.0 + k, "combine", k, 0))
+            out.append((ring_at[k] + ring_step[k] * j, "ring", k, j))
+        out.append((combine_at[k], "combine", k, 0))
     return sorted(out)
 
 

time: 107 us -> 110 us (1.028)
  Pallas kernels: 105 us -> 109 us
    pallas_call x1, Pallas kernels: 103 us -> 107 us  [local(): pl.pallas_call(kernel, out_shape=(jax.ShapeDtypeStruct((tok, model), BF16...]
where the time goes in v3:
time: 110 us
  Pallas kernels  109 us (99%)
    pallas_call x1, Pallas kernels, local(): pl.pallas_call(kernel, out_shape=(jax.ShapeDtypeStruct((tok, model), BF16...  107 us
    pallas_call x1, Pallas kernels, local(): pl.pallas_call(settle, out_shape=(jax.ShapeDtypeStruct(combined.shape, BF...  2.35 us

profile of v3, /device:TPU:6, one launch (start us, length us, event | category | flops | bytes accessed | tf_op | source)
XLA Modules:
  0.0 109.8 jit_solution(7320805744582111603)
XLA Ops:
  0.6 106.8 %moe_down.1 = (bf16[128,2048]{1,0:T(8,128)(2,1)}, bf16[384,768]{1,0:T(8,128)(2,1)}, bf16[48,2048]{1,0:T(8,128)(2,1)}) custom-call(s32[2,128]{1,0:T(2,128)} %bitcast.3, f32[2,128]{1,0:T(2,128)} %bitcast.4, bf16[384,768]{1,0:T(8,128)(2,1)} %hid_hbm.1, bf16[128,2048]{1,0:T(8,128)(2,1)} %grad_hbm.1, bf16[1,768,2048]{2,1,0:T(8,128)(2,1)} %w_hbm.1), custom_call_target="tpu_custom_call" | custom-call | tf_op jit(solution)/shard_map/moe_down/pallas_call | solution.py:390
  107.5 2.3 %settle.1 = (bf16[128,2048]{1,0:T(8,128)(2,1)}, bf16[384,768]{1,0:T(8,128)(2,1)}, bf16[48,2048]{1,0:T(8,128)(2,1)}) custom-call(bf16[128,2048]{1,0:T(8,128)(2,1)} %get-tuple-element.9.refs_0_, bf16[384,768]{1,0:T(8,128)(2,1)} %get-tuple-element.10.refs_1_, bf16[48,2048]{1,0:T(8,128)(2,1)} %get-tuple-element.11.refs_2_), custom_call_target="tpu_custom_call" | custom-call | tf_op jit(solution)/shard_map/settle/pallas_call | solution.py:431
